TPU v7x, 32 devices: a whole 2x2x4 slice. The times are simulated.
32 devices in a mesh: section: 2 (over core), dp: 16 (over z, y, x).
Axes of the slice: x: 2, y: 2, z: 4, core: 2. Of those that a mesh axis runs over, the one named last changes fastest.
Arguments:
- boundary: bfloat16 [2, 8192, 768], P('section', 'dp'), may hold values from -6 to 6
- lengths: int32 [32], P('dp'), may hold values from 64 to 256, as said below
- attn_norm_gain: bfloat16 [2, 768], P('section'), may hold values from 0.5 to 1.5
- attn_norm_bias: bfloat16 [2, 768], P('section'), may hold values from -1.75 to 1.75
- qkv_weight: bfloat16 [2, 768, 2304], P('section'), may hold values from -0.21875 to 0.21875
- qkv_bias: bfloat16 [2, 2304], P('section'), may hold values from -1.75 to 1.75
- proj_weight: bfloat16 [2, 768, 768], P('section'), may hold values from -1.25 to 1.25
- proj_bias: bfloat16 [2, 768], P('section'), may hold values from -1.75 to 1.75
- mlp_norm_gain: bfloat16 [2, 768], P('section'), may hold values from 0.5 to 1.5
- mlp_norm_bias: bfloat16 [2, 768], P('section'), may hold values from -1.75 to 1.75
- up_weight: bfloat16 [2, 768, 3072], P('section'), may hold values from -0.21875 to 0.21875
- up_bias: bfloat16 [2, 3072], P('section'), may hold values from -1.75 to 1.75
- down_weight: bfloat16 [2, 3072, 768], P('section'), may hold values from -0.109375 to 0.109375
- down_bias: bfloat16 [2, 768], P('section'), may hold values from -1.75 to 1.75
Outputs:
- boundary_out: bfloat16 [2, 8192, 768], P('section', 'dp')
- grad_attn_norm_gain: float32 [2, 768], P('section', 'dp')
- grad_attn_norm_bias: float32 [2, 768], P('section', 'dp')
- grad_qkv_weight: float32 [2, 768, 2304], P('section', 'dp')
- grad_qkv_bias: float32 [2, 2304], P('section', 'dp')
- grad_proj_weight: float32 [2, 768, 768], P('section', 'dp')
- grad_proj_bias: float32 [2, 768], P('section', 'dp')
- grad_mlp_norm_gain: float32 [2, 768], P('section', 'dp')
- grad_mlp_norm_bias: float32 [2, 768], P('section', 'dp')
- grad_up_weight: float32 [2, 768, 3072], P('section', 'dp')
- grad_up_bias: float32 [2, 3072], P('section', 'dp')
- grad_down_weight: float32 [2, 3072, 768], P('section', 'dp')
- grad_down_bias: float32 [2, 768], P('section', 'dp')
Inputs may be any that keep to these rules, and one draw needn't show every extreme that they name: `lengths`: real tokens of each sentence counted from its start; some sentence has exactly 256 and some exactly 64.
All inputs are finite; a program needn't handle non-finite values.
Results may differ from a plain program's by a relative error of at most 0.012.
Values may be sent and summed in bfloat16 or wider, within the bound.
No kernel may reach another device: no remote copies, remote signals or barrier semaphores. Data moves between devices by JAX's collectives and lax.ppermute only.
A program may use at most 192 MiB of HBM per device.

v0:
```python
import jax
import jax.numpy as jnp
from jax import lax
from jax.sharding import PartitionSpec as P

HEAD = 64


EPS = 1e-05
NEG_FILL = -1e30


def passed_along(shard, axis, by):
    count = lax.axis_size(axis)
    pairs = [(i, i + by) for i in range(count) if 0 <= i + by < count]
    return lax.ppermute(shard, axis, pairs)


def layer_norm(values, gain_vec, bias_vec):
    mean_value = jnp.mean(values, axis=-1, keepdims=True)
    centred = values - mean_value
    variance = jnp.mean(centred * centred, axis=-1, keepdims=True)
    return centred * lax.rsqrt(variance + EPS) * gain_vec + bias_vec


def gelu_erf(values):
    return 0.5 * values * (1.0 + jax.scipy.special.erf(values * 0.7071067811865476))


def rotary_tables(seq_len, head_dim):
    rot_dims = head_dim // 4
    half_rot = rot_dims // 2
    frequency = 10000.0 ** (-(jnp.arange(half_rot, dtype=jnp.float32) * 2.0 / rot_dims))
    angles = jnp.arange(seq_len, dtype=jnp.float32)[:, None] * frequency[None, :]
    return (jnp.cos(angles), jnp.sin(angles))


def rotate(values, cosine_table, sine_table, direction):
    half_rot = cosine_table.shape[1]
    first_half = values[..., :half_rot]
    second_half = values[..., half_rot : 2 * half_rot]
    cosine_part = cosine_table[:, None, :]
    sine_part = sine_table[:, None, :] * direction
    return jnp.concatenate(
        [
            first_half * cosine_part - second_half * sine_part,
            second_half * cosine_part + first_half * sine_part,
            values[..., 2 * half_rot :],
        ],
        axis=-1,
    )


def matmul(left, right):
    return jnp.dot(left, right, preferred_element_type=jnp.float32)


def left_contract(left, right):
    return lax.dot_general(
        left, right, (((0,), (0,)), ((), ())), preferred_element_type=jnp.float32
    )


def right_contract(left, right):
    return lax.dot_general(
        left, right, (((1,), (1,)), ((), ())), preferred_element_type=jnp.float32
    )


def block_scores(queries, key_rows, length, row_start, block_rows):
    scale_factor = queries.shape[-1] ** (-0.5)
    raw_scores = (
        jnp.einsum("qhe,khe->hqk", queries, key_rows, preferred_element_type=jnp.float32)
        * scale_factor
    )
    key_pos = jnp.arange(key_rows.shape[0], dtype=jnp.int32)
    query_pos = row_start + jnp.arange(block_rows, dtype=jnp.int32)
    allowed = (key_pos[None, :] <= query_pos[:, None]) & (key_pos[None, :] < length)
    return (queries, raw_scores, allowed[None])


def attend(queries, key_rows, value_rows, length):
    seq_len = queries.shape[0]
    block_rows = min(seq_len, 512)
    block_count = seq_len // block_rows

    def one_block(block_index):
        row_start = block_index * block_rows
        query_block, raw_scores, allowed = block_scores(
            queries, key_rows, length, row_start, block_rows
        )
        scores = jnp.where(allowed, raw_scores, NEG_FILL)
        row_max = jnp.max(scores, axis=-1, keepdims=True)
        exponent = jnp.exp(scores - row_max)
        row_total = jnp.sum(exponent, axis=-1, keepdims=True)
        probs_low = (exponent / row_total).astype(jnp.bfloat16)
        block_out = jnp.einsum(
            "hqk,khe->qhe", probs_low, value_rows, preferred_element_type=jnp.float32
        )
        return (block_out, (row_max + jnp.log(row_total))[..., 0])

    block_outs, log_totals = lax.map(one_block, jnp.arange(block_count, dtype=jnp.int32))
    return (block_outs.reshape(queries.shape), log_totals)


def attend_back(queries, key_rows, value_rows, length, log_totals, grad_mixed):
    seq_len = queries.shape[0]
    block_rows = min(seq_len, 512)
    block_count = seq_len // block_rows
    scale_factor = queries.shape[-1] ** (-0.5)

    def one_block(carried, block_index):
        grad_keys, grad_values = carried
        row_start = block_index * block_rows
        query_block, raw_scores, allowed = block_scores(
            queries, key_rows, length, row_start, block_rows
        )
        probs_f32 = jnp.where(
            allowed, jnp.exp(raw_scores - log_totals[block_index][..., None]), 0.0
        )
        grad_values = grad_values + jnp.einsum(
            "hqk,qhe->khe",
            probs_f32.astype(jnp.bfloat16),
            grad_mixed,
            preferred_element_type=jnp.float32,
        )
        grad_probs = jnp.einsum(
            "qhe,khe->hqk", grad_mixed, value_rows, preferred_element_type=jnp.float32
        )
        inner_sum = jnp.sum(probs_f32 * grad_probs, axis=-1, keepdims=True)
        grad_scores = (probs_f32 * (grad_probs - inner_sum)).astype(jnp.bfloat16)
        grad_query = (
            jnp.einsum("hqk,khe->qhe", grad_scores, key_rows, preferred_element_type=jnp.float32)
            * scale_factor
        )
        grad_keys = (
            grad_keys
            + jnp.einsum(
                "hqk,qhe->khe", grad_scores, query_block, preferred_element_type=jnp.float32
            )
            * scale_factor
        )
        return ((grad_keys, grad_values), grad_query)

    zero_rows = jnp.zeros(queries.shape, jnp.float32)
    (grad_keys, grad_values), grad_queries = lax.scan(
        one_block, (zero_rows, zero_rows), jnp.arange(block_count, dtype=jnp.int32)
    )
    return (grad_queries.reshape(queries.shape), grad_keys, grad_values)


def layer_forward(inputs, length, params, tables):
    (
        gain_a,
        shift_a,
        weight_qkv,
        bias_qkv,
        weight_proj,
        bias_proj,
        gain_b,
        shift_b,
        weight_up,
        bias_up,
        weight_down,
        bias_down,
    ) = params
    seq_len, width = inputs.shape
    head_count = width // HEAD
    cosine_table, sine_table = tables
    residual = inputs.astype(jnp.float32)
    normed_a = layer_norm(residual, gain_a.astype(jnp.float32), shift_a.astype(jnp.float32)).astype(
        jnp.bfloat16
    )
    packed = (matmul(normed_a, weight_qkv) + bias_qkv.astype(jnp.float32)).reshape(
        seq_len, 3, head_count, HEAD
    )
    queries = rotate(packed[:, 0], cosine_table, sine_table, 1.0).astype(jnp.bfloat16)
    key_rows = rotate(packed[:, 1], cosine_table, sine_table, 1.0).astype(jnp.bfloat16)
    value_rows = packed[:, 2].astype(jnp.bfloat16)
    attended, log_totals = attend(queries, key_rows, value_rows, length)
    mixed_heads = attended.reshape(seq_len, width).astype(jnp.bfloat16)
    normed_b = layer_norm(residual, gain_b.astype(jnp.float32), shift_b.astype(jnp.float32)).astype(
        jnp.bfloat16
    )
    up_proj = matmul(normed_b, weight_up) + bias_up.astype(jnp.float32)
    hidden = gelu_erf(up_proj).astype(jnp.bfloat16)
    branch = (
        matmul(mixed_heads, weight_proj)
        + bias_proj.astype(jnp.float32)
        + matmul(hidden, weight_down)
        + bias_down.astype(jnp.float32)
    )
    saved_parts = (
        residual,
        normed_a,
        queries,
        key_rows,
        value_rows,
        log_totals,
        mixed_heads,
        normed_b,
        up_proj,
        hidden,
    )
    return (residual + branch, saved_parts)


def layer_backward(saved_parts, grad_low, length, params, tables, is_valid):
    (
        gain_a,
        shift_a,
        weight_qkv,
        bias_qkv,
        weight_proj,
        bias_proj,
        gain_b,
        shift_b,
        weight_up,
        bias_up,
        weight_down,
        bias_down,
    ) = params
    (
        residual,
        normed_a,
        queries,
        key_rows,
        value_rows,
        log_totals,
        mixed_heads,
        normed_b,
        up_proj,
        hidden,
    ) = saved_parts
    seq_len, width = residual.shape
    cosine_table, sine_table = tables
    grad_wide = grad_low.astype(jnp.float32)
    column_sum = jnp.sum(grad_wide, axis=0) * is_valid
    grad_proj_w = left_contract(mixed_heads, grad_low) * is_valid
    grad_down_w = left_contract(hidden, grad_low) * is_valid
    grad_hidden = right_contract(grad_low, weight_down)
    gelu_back = jax.vjp(gelu_erf, up_proj)[1]
    grad_up_proj = gelu_back(grad_hidden)[0].astype(jnp.bfloat16)
    grad_up_w = left_contract(normed_b, grad_up_proj) * is_valid
    grad_up_b = jnp.sum(grad_up_proj, axis=0, dtype=jnp.float32) * is_valid
    early_sums = None
    grad_normed_b = right_contract(grad_up_proj, weight_up)
    grad_mixed = right_contract(grad_low, weight_proj).astype(jnp.bfloat16).reshape(queries.shape)
    grad_queries, grad_keys, grad_values = attend_back(
        queries, key_rows, value_rows, length, log_totals, grad_mixed
    )
    grad_queries = rotate(grad_queries, cosine_table, sine_table, -1.0)
    grad_keys = rotate(grad_keys, cosine_table, sine_table, -1.0)
    grad_packed = jnp.stack([grad_queries, grad_keys, grad_values], axis=1)
    grad_packed = grad_packed.reshape(seq_len, 3 * width).astype(jnp.bfloat16)
    grad_qkv_w = left_contract(normed_a, grad_packed) * is_valid
    grad_qkv_b = jnp.sum(grad_packed, axis=0, dtype=jnp.float32) * is_valid
    grad_normed_a = right_contract(grad_packed, weight_qkv)
    norm_back_a = jax.vjp(
        layer_norm, residual, gain_a.astype(jnp.float32), shift_a.astype(jnp.float32)
    )[1]
    grad_res_a, grad_gain_a, grad_shift_a = norm_back_a(grad_normed_a)
    norm_back_b = jax.vjp(
        layer_norm, residual, gain_b.astype(jnp.float32), shift_b.astype(jnp.float32)
    )[1]
    grad_res_b, grad_gain_b, grad_shift_b = norm_back_b(grad_normed_b)
    grad_input = grad_wide + grad_res_a + grad_res_b
    layer_grads = (
        grad_gain_a * is_valid,
        grad_shift_a * is_valid,
        grad_qkv_w,
        grad_qkv_b,
        grad_proj_w,
        column_sum,
        grad_gain_b * is_valid,
        grad_shift_b * is_valid,
        grad_up_w,
        grad_up_b,
        grad_down_w,
        column_sum,
    )
    return (grad_input, layer_grads, early_sums)


def per_device(
    boundary,
    lengths,
    attn_norm_gain,
    attn_norm_bias,
    qkv_weight,
    qkv_bias,
    proj_weight,
    proj_bias,
    mlp_norm_gain,
    mlp_norm_bias,
    up_weight,
    up_bias,
    down_weight,
    down_bias,
):
    params = (
        attn_norm_gain[0],
        attn_norm_bias[0],
        qkv_weight[0],
        qkv_bias[0],
        proj_weight[0],
        proj_bias[0],
        mlp_norm_gain[0],
        mlp_norm_bias[0],
        up_weight[0],
        up_bias[0],
        down_weight[0],
        down_bias[0],
    )
    section_index = lax.axis_index("section")
    is_first = section_index == 0
    batches = lengths.shape[0]
    width = boundary.shape[2]
    seq_len = boundary.shape[1] // batches
    local_rows = boundary[0].reshape(batches, seq_len, width)
    tables = rotary_tables(seq_len, HEAD)
    stashed = []
    kept = []
    finals = []
    previous = jnp.zeros((seq_len, width), jnp.bfloat16)
    for tick_number in range(batches + 1):
        own_rows = local_rows[min(tick_number, batches - 1)]
        if tick_number == 0:
            arriving = jnp.zeros_like(own_rows)
        else:
            arriving = passed_along(previous, "section", 1)
        inputs = jnp.where(is_first, own_rows, arriving)
        length = lengths[jnp.clip(tick_number - section_index, 0, batches - 1)]
        result, saved_parts = layer_forward(inputs, length, params, tables)
        previous = result.astype(jnp.bfloat16)
        stashed.append((inputs, length))
        kept.append(saved_parts)
        finals.append(previous)
    totals = [jnp.zeros(piece.shape, jnp.float32) for piece in params]
    input_grads = []
    grad_prev = jnp.zeros((seq_len, width), jnp.bfloat16)
    for tick_number in range(batches + 1):
        cotangent = local_rows[min(tick_number, batches - 1)]
        if tick_number == 0:
            arriving = jnp.zeros_like(cotangent)
        else:
            arriving = passed_along(grad_prev, "section", -1)
        incoming = jnp.where(is_first, arriving, cotangent)
        early = max(tick_number - 1, 0)
        late = min(tick_number + 1, batches)
        length = jnp.where(is_first, stashed[early][1], stashed[late][1])
        inputs = jnp.where(is_first, stashed[early][0], stashed[late][0])
        saved_parts = layer_forward(inputs, length, params, tables)[1]
        is_valid = jnp.where(is_first, tick_number >= 1, tick_number < batches).astype(jnp.float32)
        grad_input, layer_grads, early_result = layer_backward(
            saved_parts, incoming, length, params, tables, is_valid
        )
        totals = [older + newer for older, newer in zip(totals, layer_grads)]
        grad_prev = grad_input.astype(jnp.bfloat16)
        input_grads.append(grad_prev)
    shares = (
        lax.psum_scatter(totals[0], "dp", scatter_dimension=0, tiled=True),
        lax.psum_scatter(totals[1], "dp", scatter_dimension=0, tiled=True),
        lax.psum_scatter(totals[2], "dp", scatter_dimension=0, tiled=True),
        lax.psum_scatter(totals[3], "dp", scatter_dimension=0, tiled=True),
        lax.psum_scatter(totals[4], "dp", scatter_dimension=0, tiled=True),
        lax.psum_scatter(totals[5], "dp", scatter_dimension=0, tiled=True),
        lax.psum_scatter(totals[6], "dp", scatter_dimension=0, tiled=True),
        lax.psum_scatter(totals[7], "dp", scatter_dimension=0, tiled=True),
        lax.psum_scatter(totals[8], "dp", scatter_dimension=0, tiled=True),
        lax.psum_scatter(totals[9], "dp", scatter_dimension=0, tiled=True),
        lax.psum_scatter(totals[10], "dp", scatter_dimension=0, tiled=True),
        lax.psum_scatter(totals[11], "dp", scatter_dimension=0, tiled=True),
    )
    joined = jnp.where(
        is_first, jnp.concatenate(input_grads[1:], axis=0), jnp.concatenate(finals[1:], axis=0)
    )
    boundary_out = joined[None]
    return (
        boundary_out,
        shares[0][None],
        shares[1][None],
        shares[2][None],
        shares[3][None],
        shares[4][None],
        shares[5][None],
        shares[6][None],
        shares[7][None],
        shares[8][None],
        shares[9][None],
        shares[10][None],
        shares[11][None],
    )


def solution(mesh):
    placed = (
        P("section", "dp", None),
        P("dp"),
        P("section", None),
        P("section", None),
        P("section", None, None),
        P("section", None),
        P("section", None, None),
        P("section", None),
        P("section", None),
        P("section", None),
        P("section", None, None),
        P("section", None),
        P("section", None, None),
        P("section", None),
    )
    return jax.shard_map(
        per_device,
        mesh=mesh,
        in_specs=placed,
        out_specs=(
            P("section", "dp", None),
            P("section", "dp"),
            P("section", "dp"),
            P("section", "dp", None),
            P("section", "dp"),
            P("section", "dp", None),
            P("section", "dp"),
            P("section", "dp"),
            P("section", "dp"),
            P("section", "dp", None),
            P("section", "dp"),
            P("section", "dp", None),
            P("section", "dp"),
        ),
        check_vma=False,
    )
```

profile of v0, /device:TPU:0, one launch (start us, length us, event | category | flops | bytes accessed | tf_op | source)
XLA Modules:
  0.0 844.1 jit_solution(6464191178029386081)
XLA Ops:
  16.7 3.7 convolution_add_fusion.5
  20.4 3.1 copy.90
  28.0 2.3 fusion.151
  30.3 7.8 fusion.13
  38.1 3.0 fusion.146
  41.1 3.4 collective-permute-start
  49.7 2.7 convolution_convert_fusion.2
  55.2 7.8 fusion.9
  62.9 3.6 convolution_add_fusion.3
  66.5 3.1 copy.97
  76.1 2.5 collective-permute-start.2
  87.5 2.6 convolution_add_fusion.4
  90.2 5.5 fusion.36
  97.9 2.6 convolution_add_fusion
  100.5 3.0 copy.109
  103.5 2.7 slice_bitcast_fusion
  106.3 2.6 convolution_add_fusion.2
  108.9 3.1 copy.99
  115.8 3.1 copy.92
  123.9 2.6 convolution_add_fusion.1
  126.5 3.2 copy.104
  131.4 1.9 subtract_convert_fusion.1
  135.8 2.9 fusion.153
  147.0 3.4 convert_reduce_fusion.2
  153.3 3.2 fusion.152
  163.5 3.2 fusion.42
  171.4 2.8 fusion.125
  174.4 2.3 multiply_reduce_fusion.1
  179.8 3.3 convert_reduce_fusion.1
  198.1 5.7 fusion.424
  203.8 4.3 fusion.418
  211.3 3.5 multiply_reduce_fusion
  221.1 4.5 multiply_add_fusion.2
  226.3 5.9 fusion.45
  236.0 6.3 multiply_add_fusion
  242.9 3.3 fusion.421
  248.3 5.3 convert_reduce_fusion
  254.8 5.4 multiply_add_fusion.1
  269.0 2.3 fusion.149
  271.4 7.8 fusion.3
  279.1 3.1 fusion.155
  284.3 4.4 fusion.17
  295.3 79.5 %all-reduce.7 = (f32[768]{0:T(1024)}, f32[768]{0:T(1024)}, f32[2304]{0:T(1024)}, f32[768]{0:T(1024)}, f32[768]{0:T(1024)}, /*index=5*/f32[768]{0:T(1024)}, f32[3072]{0:T(1024)}) all-reduce(f32[768]{0:T(1024)} %multiply_add_fusion.16, f32[768]{0:T(1024)} %multiply_add_fusion.15, ...), channel_id=2, replica_groups=mesh['section'=2,'dp'=16] {'dp'}, use_global_device_ids=true, to_apply=%region_42.43.clone | all-reduce | flops 9216 | bytes 73728
  385.1 2.2 fusion.265
  387.3 2.3 maximum_select_fusion
  389.6 93.1 %reduce-scatter.5.cloned.1.call-done = f32[48,2304]{1,0:T(8,128)} async-done(((f32[768,2304]{1,0:T(8,128)}), f32[48,2304]{1,0:T(8,128)}) %reduce-scatter.5.cloned.1.call-update) | async-done | bytes 442384 | tf_op jit(solution)/shard_map/reduce_scatter | solution.py:364
  482.7 177.0 %reduce-scatter.11.cloned.1.call-done = f32[192,768]{1,0:T(8,128)} async-done(((f32[3072,768]{1,0:T(8,128)}), f32[192,768]{1,0:T(8,128)}) %reduce-scatter.11.cloned.1.call-update) | async-done | bytes 589840 | tf_op jit(solution)/shard_map/reduce_scatter | solution.py:372
  659.7 176.3 %reduce-scatter.9.cloned.1.call-done = f32[48,3072]{1,0:T(8,128)} async-done(((f32[768,3072]{1,0:T(8,128)}), f32[48,3072]{1,0:T(8,128)}) %reduce-scatter.9.cloned.1.call-update) | async-done | bytes 589840 | tf_op jit(solution)/shard_map/reduce_scatter | solution.py:370
  (576 shorter events, 132.5 us)
Async XLA Ops:
  7.2 9.5 %copy-start = (bf16[1,768,2304]{2,1,0:T(8,128)(2,1)S(1)}, bf16[1,768,2304]{2,1,0:T(8,128)(2,1)}, u32[]{:S(2)}) copy-start(bf16[1,768,2304]{2,1,0:T(8,128)(2,1)} %param.18) | copy-start | bytes 10616836
  7.2 382.4 %reduce-scatter.7.cloned.1.call-start = ((), (), s32[]{:S(2)}) async-start(), calls=%async_computation.5 | async-start | bytes 2506752 | tf_op jit(solution)/shard_map/reduce_scatter | solution.py:366
  10.5 6.1 copy-start.169
  41.1 11.3 %collective-permute-start = (bf16[256,768]{1,0:T(8,128)(2,1)}, bf16[256,768]{1,0:T(8,128)(2,1)}, u32[]{:S(2)}, u32[]{:S(2)}) collective-permute-start(bf16[256,768]{1,0:T(8,128)(2,1)} %fusion.146), channel_id=1, source_target_pairs={{0,16},{1,17},{2,18},{3,19},{4,20},{5,21},{6,22},{7,23},{8,24},{9,... | collective-permute-start | bytes 1179656 | tf_op jit(solution)/shard_map/ppermute | solution.py:16
  76.1 7.3 collective-permute-start.2
  82.7 4.8 copy-start.73
  82.7 4.8 copy-start.156
  84.6 12.7 %copy-start.49 = (bf16[256,768]{1,0:T(8,128)(2,1)}, bf16[256,768]{1,0:T(8,128)(2,1)S(1)}, u32[]{:S(2)}) copy-start(bf16[256,768]{1,0:T(8,128)(2,1)S(1)} %get-tuple-element.260) | copy-start | bytes 1179652
  84.6 12.7 %copy-start.168 = (f32[256]{0:T(256)}, f32[256]{0:T(256)S(1)}, u32[]{:S(2)}) copy-start(f32[256]{0:T(256)S(1)} %broadcast_multiply_fusion.1) | copy-start | bytes 3076
  86.5 9.1 %copy-start.16 = (bf16[256,768]{1,0:T(8,128)(2,1)}, bf16[256,768]{1,0:T(8,128)(2,1)S(1)}, u32[]{:S(2)}) copy-start(bf16[256,768]{1,0:T(8,128)(2,1)S(1)} %get-tuple-element.336) | copy-start | bytes 1179652
  86.5 9.9 %copy-start.8 = (bf16[256,768]{1,0:T(8,128)(2,1)}, bf16[256,768]{1,0:T(8,128)(2,1)S(1)}, u32[]{:S(2)}) copy-start(bf16[256,768]{1,0:T(8,128)(2,1)S(1)} %get-tuple-element.278) | copy-start | bytes 1179652
  118.9 4.9 copy-start.17
  118.9 4.9 copy-start.75
  118.9 4.9 copy-start.137
  118.9 4.9 copy-start.140
  119.0 4.9 copy-start.158
  131.4 20.5 %copy-start.59 = (bf16[256,12,48]{0,2,1:T(8,128)(2,1)}, bf16[256,12,48]{0,2,1:T(8,128)(2,1)S(1)}, u32[]{:S(2)}) copy-start(bf16[256,12,48]{0,2,1:T(8,128)(2,1)S(1)} %slice.556) | copy-start | bytes 884740
  131.4 20.5 %copy-start.57 = (bf16[256,12,48]{0,2,1:T(8,128)(2,1)}, bf16[256,12,48]{0,2,1:T(8,128)(2,1)S(1)}, u32[]{:S(2)}) copy-start(bf16[256,12,48]{0,2,1:T(8,128)(2,1)S(1)} %slice.557) | copy-start | bytes 884740
  133.4 18.5 %copy-start.88 = (bf16[256,12,8]{0,2,1:T(8,128)(2,1)}, bf16[256,12,8]{0,2,1:T(8,128)(2,1)S(1)}, u32[]{:S(2)}) copy-start(bf16[256,12,8]{0,2,1:T(8,128)(2,1)S(1)} %get-tuple-element.352) | copy-start | bytes 147460
  133.4 18.5 %copy-start.90 = (bf16[256,12,8]{0,2,1:T(8,128)(2,1)}, bf16[256,12,8]{0,2,1:T(8,128)(2,1)S(1)}, u32[]{:S(2)}) copy-start(bf16[256,12,8]{0,2,1:T(8,128)(2,1)S(1)} %get-tuple-element.353) | copy-start | bytes 147460
  133.4 18.5 %copy-start.92 = (bf16[256,12,8]{0,2,1:T(8,128)(2,1)}, bf16[256,12,8]{0,2,1:T(8,128)(2,1)S(1)}, u32[]{:S(2)}) copy-start(bf16[256,12,8]{0,2,1:T(8,128)(2,1)S(1)} %get-tuple-element.354) | copy-start | bytes 147460
  133.4 18.5 %copy-start.94 = (bf16[256,12,8]{0,2,1:T(8,128)(2,1)}, bf16[256,12,8]{0,2,1:T(8,128)(2,1)S(1)}, u32[]{:S(2)}) copy-start(bf16[256,12,8]{0,2,1:T(8,128)(2,1)S(1)} %get-tuple-element.355) | copy-start | bytes 147460
  144.8 5.6 slice-start.8
  161.6 6.6 copy-start.39
  161.6 5.1 collective-permute-start.1
  178.4 4.8 slice-start.10
  189.5 3.6 collective-permute-start.3
  196.5 286.2 %reduce-scatter.5.cloned.1.call-start = ((), (), s32[]{:S(2)}) async-start(), calls=%async_computation.4 | async-start | bytes 7520256 | tf_op jit(solution)/shard_map/reduce_scatter | solution.py:364
  198.1 5.7 copy-start.12
  198.1 5.7 copy-start.37
  198.1 5.7 copy-start.76
  198.1 5.7 copy-start.127
  198.1 5.7 copy-start.134
  214.9 5.6 slice-start.2
  225.6 434.1 %reduce-scatter.11.cloned.1.call-start = ((), (), s32[]{:S(2)}) async-start(), calls=%async_computation.7 | async-start | bytes 10027008 | tf_op jit(solution)/shard_map/reduce_scatter | solution.py:372
  226.3 5.9 copy-start.7
  226.3 5.9 copy-start.30
  242.3 593.7 %reduce-scatter.9.cloned.1.call-start = ((), (), s32[]{:S(2)}) async-start(), calls=%async_computation.6 | async-start | bytes 10027008 | tf_op jit(solution)/shard_map/reduce_scatter | solution.py:370
  248.3 6.5 copy-start.19
  248.3 6.5 copy-start.139
  248.3 6.5 copy-start.142
  288.8 4.7 copy-start.146
  288.8 4.7 copy-start.149
  288.8 5.3 copy-start.145
  288.8 5.3 copy-start.148
  288.8 5.9 copy-start.153
  288.8 5.9 copy-start.154
  288.8 5.9 copy-start.159
  (157 other events, 383.9 us)
Sparse Core Ops, SparseCore 0:
  196.7 129.6 reduce-scatter.6
  333.1 149.5 reduce-scatter.4
  490.0 169.7 reduce-scatter.10
  665.8 170.0 reduce-scatter.8
where the time goes:
time: 852 us; the launch traced here: 844 us
  waiting for transfers between devices  448 us (53%)
  matrix products  163 us (19%)
  blocking collectives  79.5 us (9%)
  local copies, waits for them, and re-layouts  67 us (8%)
  other arithmetic  54.7 us (6%)
  between operations  22.6 us (3%)
  starting transfers between devices  9.6 us (1%)
    reduce_scatter x1, waiting for transfers between devices, per_device(): lax.psum_scatter(totals[10], 'dp', scatter_dimension=0, tiled=True)  177 us
    reduce_scatter x1, waiting for transfers between devices, per_device(): lax.psum_scatter(totals[8], 'dp', scatter_dimension=0, tiled=True)  176 us
    reduce_scatter x1, waiting for transfers between devices, per_device(): lax.psum_scatter(totals[2], 'dp', scatter_dimension=0, tiled=True)  93.1 us
    unnamed x1, blocking collectives  79.5 us
    dot_general x15, matrix products, matmul(): return jnp.dot(left, right, preferred_element_type=jnp.float32)  63 us
    dot_general x12, matrix products, left_contract(): lax.dot_general(left, right, (((0,), (0,)), ((), ())), preferred_element_...  37.4 us
    dot_general x12, matrix products, right_contract(): lax.dot_general(left, right, (((1,), (1,)), ((), ())), preferred_element_...  29.6 us
    add x6, local copies, waits for them, and re-layouts, layer_forward(): matmul(normed_a, weight_qkv) + bias_qkv.astype(jnp.float32)  18.6 us
  transfers between devices with their start and end apart: 8, of which 4 were waited for; matrix products, arithmetic and copies ran while one was open for 14% of the time, Pallas kernels for 0%

commit v1 on v0

v1 whole, which is shorter than its diff:
```python
import functools
import math

import jax
import jax.numpy as jnp
import numpy as np
from jax import lax
from jax.experimental import pallas as pl
from jax.experimental.pallas import tpu as pltpu
from jax.sharding import PartitionSpec as P

HEAD = 64
EPS = 1e-05
NEG_FILL = -1e30
VMEM_BYTES = 56 * 1024 * 1024
F32 = jnp.float32
BF16 = jnp.bfloat16


def dot(left, right):
    return jnp.dot(left, right, preferred_element_type=F32)


def dot_nt(left, right):
    return lax.dot_general(left, right, (((1,), (1,)), ((), ())), preferred_element_type=F32)


def normalised(values):
    centred = values - jnp.mean(values, axis=-1, keepdims=True)
    variance = jnp.mean(centred * centred, axis=-1, keepdims=True)
    scale = lax.rsqrt(variance + EPS)
    return centred * scale, scale


def gelu_parts(values):
    bell = jnp.exp(values * values * -0.5)
    t = 1.0 / (1.0 + (0.3275911 * math.sqrt(0.5)) * jnp.abs(values))
    poly = 0.5 * 1.061405429
    for coefficient in (-1.453152027, 1.421413741, -0.284496736, 0.254829592):
        poly = poly * t + 0.5 * coefficient
    tail = poly * t * bell
    integral = jnp.where(values >= 0.0, 1.0 - tail, tail)
    return values * integral, integral + values * bell * (1.0 / math.sqrt(2.0 * math.pi))


def rotary_lanes(seq_len, lanes):
    rot_dims = HEAD // 4
    half = rot_dims // 2
    frequency = np.float32(10000.0) ** (-(np.arange(half, dtype=np.float32) * np.float32(2.0) / np.float32(rot_dims)))
    angles = np.arange(seq_len, dtype=np.float32)[:, None] * frequency.astype(np.float32)[None, :]
    cosine, sine = np.cos(angles).astype(np.float32), np.sin(angles).astype(np.float32)
    same = np.ones((seq_len, HEAD), np.float32)
    later = np.zeros((seq_len, HEAD), np.float32)
    earlier = np.zeros((seq_len, HEAD), np.float32)
    same[:, :half] = cosine
    same[:, half:rot_dims] = cosine
    later[:, :half] = -sine
    earlier[:, half:rot_dims] = sine
    return [np.tile(t, (1, lanes // HEAD)) for t in (same, later, earlier)]


def turned(values, same, later, earlier, sign):
    half = HEAD // 8
    width = values.shape[1]
    ahead = pltpu.roll(values, width - half, 1)
    behind = pltpu.roll(values, half, 1)
    if sign > 0:
        return values * same + ahead * later + behind * earlier
    return values * same - ahead * later - behind * earlier


def forward_kernel(
    groups, scalars, own, arriving, gain_a, shift_a, gain_b, shift_b, wq, wk, wv, bq, bk, bv, wp, bp, wu, bu, wd, bd,
    same, later, earlier,
    y_out, x_out, na_out, nb_out, q_out, k_out, v_out, pt_out, mixed_out, hidden_out, slope_out, total,
):
    step = pl.program_id(0)
    length = scalars[2]

    @pl.when(step == 0)
    def _():
        x_low = jnp.where(scalars[1] == 1, own[0], arriving[...])
        x_out[0] = x_low
        x = x_low.astype(F32)
        xhat, _ = normalised(x)
        na_out[0] = (xhat * gain_a[...].astype(F32) + shift_a[...].astype(F32)).astype(BF16)
        nb_out[0] = (xhat * gain_b[...].astype(F32) + shift_b[...].astype(F32)).astype(BF16)
        total[...] = x + (bp[...].astype(F32) + bd[...].astype(F32))

    rows = na_out.shape[1]
    na = na_out[0]
    tables = (same[...], later[...], earlier[...])
    q8 = (turned(dot(na, wq[0]) + bq[...].astype(F32), *tables, 1) * (HEAD**-0.5)).astype(BF16)
    k = turned(dot(na, wk[0]) + bk[...].astype(F32), *tables, 1).astype(BF16)
    v = (dot(na, wv[0]) + bv[...].astype(F32)).astype(BF16)
    q_out[0] = q8
    k_out[0] = k
    v_out[0] = v
    vt = v.T
    key_pos = lax.broadcasted_iota(jnp.int32, (rows, rows), 0)
    query_pos = lax.broadcasted_iota(jnp.int32, (rows, rows), 1)
    bias = jnp.where((key_pos <= query_pos) & (key_pos < length), 0.0, NEG_FILL)
    lane = lax.broadcasted_iota(jnp.int32, (rows, 2 * HEAD), 1)
    heads = q8.shape[1] // HEAD
    mixed_t = []
    for head in range(heads):
        pair = slice(head // 2 * 2 * HEAD, head // 2 * 2 * HEAD + 2 * HEAD)
        k_one = jnp.where((lane < HEAD) == (head % 2 == 0), k[:, pair], jnp.zeros_like(k[:, pair]))
        scores = dot_nt(k_one, q8[:, pair]) + bias
        exponent = jnp.exp(scores - jnp.max(scores, axis=0, keepdims=True))
        pt = (exponent * (1.0 / jnp.sum(exponent, axis=0, keepdims=True))).astype(BF16)
        pt_out[0, head] = pt
        mixed_t.append(dot(vt[head * HEAD : head * HEAD + HEAD], pt))
    mixed = jnp.concatenate(mixed_t, axis=0).T.astype(BF16)
    mixed_out[0] = mixed
    up = dot(nb_out[0], wu[0]) + bu[...].astype(F32)
    hidden, slope = gelu_parts(up)
    hidden = hidden.astype(BF16)
    hidden_out[0] = hidden
    slope_out[0] = slope.astype(BF16)
    total[...] += dot(mixed, wp[0]) + dot(hidden, wd[0])

    @pl.when(step == groups - 1)
    def _():
        y_out[...] = total[...].astype(BF16)


def backward_kernel(
    groups, scalars, own, arriving, x_in, gain_a, gain_b, wq, wk, wv, wp, wu, wd, same, later, earlier,
    q_in, k_in, v_in, pt_in, slope_in,
    gx_out, gy_out, gq_out, gk_out, gv_out, gu_out, vec_out, total_a, total_b,
):
    step = pl.program_id(0)

    @pl.when(step == 0)
    def _():
        gy_out[0] = jnp.where(scalars[1] == 1, arriving[...], own[0])
        total_a[...] = jnp.zeros_like(total_a)
        total_b[...] = jnp.zeros_like(total_b)

    rows = gy_out.shape[1]
    gy = gy_out[0]
    grad_hidden = dot_nt(gy, wd[0])
    gu = (grad_hidden * slope_in[0].astype(F32)).astype(BF16)
    gu_out[0] = gu
    total_b[...] += dot_nt(gu, wu[0])
    gm = dot_nt(gy, wp[0]).astype(BF16)
    q8, k, v = q_in[0], k_in[0], v_in[0]
    kt = k.T
    lane = lax.broadcasted_iota(jnp.int32, (rows, 2 * HEAD), 1)
    heads = q8.shape[1] // HEAD
    gq_t, gk_parts, gv_parts = [], [], []
    for pair_index in range(heads // 2):
        pair = slice(pair_index * 2 * HEAD, pair_index * 2 * HEAD + 2 * HEAD)
        gk_pair, gv_pair = None, None
        for side in range(2):
            head = pair_index * 2 + side
            here = (lane < HEAD) == (side == 0)
            gm_one = jnp.where(here, gm[:, pair], jnp.zeros_like(gm[:, pair]))
            q_one = jnp.where(here, q8[:, pair], jnp.zeros_like(q8[:, pair]))
            pt = pt_in[0, head]
            gp = dot_nt(v[:, pair], gm_one)
            weighted = pt.astype(F32) * gp
            inner = jnp.sum(weighted, axis=0, keepdims=True)
            gs = (weighted - pt.astype(F32) * inner).astype(BF16)
            gv_one = dot(pt, gm_one)
            gk_one = dot(gs, q_one)
            gq_t.append(dot(kt[head * HEAD : head * HEAD + HEAD], gs))
            gv_pair = gv_one if gv_pair is None else gv_pair + gv_one
            gk_pair = gk_one if gk_pair is None else gk_pair + gk_one
        gk_parts.append(gk_pair)
        gv_parts.append(gv_pair)
    tables = (same[...], later[...], earlier[...])
    gq = jnp.concatenate(gq_t, axis=0).T * (HEAD**-0.5)
    gq = turned(gq, *tables, -1).astype(BF16)
    gk = turned(jnp.concatenate(gk_parts, axis=1), *tables, -1).astype(BF16)
    gv = jnp.concatenate(gv_parts, axis=1).astype(BF16)
    gq_out[0] = gq
    gk_out[0] = gk
    gv_out[0] = gv
    total_a[...] += dot_nt(gq, wq[0]) + dot_nt(gk, wk[0]) + dot_nt(gv, wv[0])

    @pl.when(step == groups - 1)
    def _():
        xhat, scale = normalised(x_in[0].astype(F32))
        grad_a, grad_b = total_a[...], total_b[...]
        sums = [jnp.sum(t, axis=0, keepdims=True) for t in (grad_a * xhat, grad_a, grad_b * xhat, grad_b)]
        vec_out[0] = jnp.concatenate(sums + [jnp.zeros((4, sums[0].shape[1]), F32)], axis=0)
        both = grad_a * gain_a[...].astype(F32) + grad_b * gain_b[...].astype(F32)
        inner = jnp.mean(both * xhat, axis=-1, keepdims=True)
        gx = gy.astype(F32) + scale * (both - jnp.mean(both, axis=-1, keepdims=True) - xhat * inner)
        gx_out[...] = gx.astype(BF16)


def whole(shape):
    return pl.BlockSpec(shape, lambda g, s: (0,) * len(shape))


def slot_whole(*shape):
    return pl.BlockSpec((1,) + shape, lambda g, s: (s[0],) + (0,) * len(shape))


def slot_columns(rows, columns):
    return pl.BlockSpec((1, rows, columns), lambda g, s: (s[0], 0, g))


def section_columns(rows, columns, offset=0):
    return pl.BlockSpec((1, rows, columns), lambda g, s: (0, 0, offset + g))


def vector_columns(columns, offset=0):
    return pl.BlockSpec((1, columns), lambda g, s: (0, offset + g))


def section_rows(rows, columns):
    return pl.BlockSpec((1, rows, columns), lambda g, s: (0, g, 0))


def sizes(params, rows):
    width = params[0].shape[1]
    units = params[8].shape[2]
    groups = width // 256
    return width, units, groups, width // groups, units // groups


def forward_tick(scalars, local_rows, arriving, params, tables, saved):
    (gain_a, shift_a, w_qkv, b_qkv, w_proj, b_proj, gain_b, shift_b, w_up, b_up, w_down, b_down) = params
    slots, rows, width = local_rows.shape
    width, units, groups, lanes, chunk = sizes(params, rows)
    heads = width // HEAD
    per = heads // groups
    in_specs = [
        slot_whole(rows, width), whole((rows, width)), whole((1, width)), whole((1, width)), whole((1, width)), whole((1, width)),
        section_columns(width, lanes), section_columns(width, lanes, groups), section_columns(width, lanes, 2 * groups),
        vector_columns(lanes), vector_columns(lanes, groups), vector_columns(lanes, 2 * groups),
        section_rows(lanes, width), whole((1, width)),
        section_columns(width, chunk), vector_columns(chunk), section_rows(chunk, width), whole((1, width)),
    ] + [whole((rows, lanes))] * 3
    operands = [
        local_rows, arriving, gain_a, shift_a, gain_b, shift_b, w_qkv, w_qkv, w_qkv, b_qkv, b_qkv, b_qkv, w_proj, b_proj,
        w_up, b_up, w_down, b_down,
    ] + list(tables)
    out_specs = [
        whole((rows, width)), slot_whole(rows, width), slot_whole(rows, width), slot_whole(rows, width),
        slot_columns(rows, lanes), slot_columns(rows, lanes), slot_columns(rows, lanes),
        pl.BlockSpec((1, per, rows, rows), lambda g, s: (s[0], g, 0, 0)),
        slot_columns(rows, lanes), slot_columns(rows, chunk), slot_columns(rows, chunk),
    ]
    out_shape = [jax.ShapeDtypeStruct((rows, width), BF16)] + [jax.ShapeDtypeStruct((slots, rows, width), BF16)] * 6 + [
        jax.ShapeDtypeStruct((slots, heads, rows, rows), BF16),
        jax.ShapeDtypeStruct((slots, rows, width), BF16),
        jax.ShapeDtypeStruct((slots, rows, units), BF16),
        jax.ShapeDtypeStruct((slots, rows, units), BF16),
    ]
    aliases = {}
    kernel = functools.partial(forward_kernel, groups)
    if saved is not None:
        count = len(operands)
        inner = kernel

        def kernel(scalars, *refs):
            return inner(scalars, *refs[:count], *refs[count + len(saved):])

        in_specs = in_specs + [pl.BlockSpec(memory_space=pl.ANY)] * len(saved)
        operands = operands + list(saved)
        aliases = {1 + count + i: 1 + i for i in range(len(saved))}
    outs = pl.pallas_call(
        kernel,
        grid_spec=pltpu.PrefetchScalarGridSpec(
            num_scalar_prefetch=1, grid=(groups,), in_specs=in_specs, out_specs=out_specs,
            scratch_shapes=[pltpu.VMEM((rows, width), F32)],
        ),
        out_shape=out_shape,
        input_output_aliases=aliases,
        compiler_params=pltpu.CompilerParams(vmem_limit_bytes=VMEM_BYTES),
        cost_estimate=pl.CostEstimate(flops=2 * rows * (4 * width * width + 2 * width * units), bytes_accessed=22 << 20, transcendentals=0),
        name="layer_forward",
    )(scalars, *operands)
    return outs[0], outs[1:]


def backward_tick(scalars, local_rows, arriving, params, tables, saved, grads):
    (gain_a, shift_a, w_qkv, b_qkv, w_proj, b_proj, gain_b, shift_b, w_up, b_up, w_down, b_down) = params
    x_s, na_s, nb_s, q_s, k_s, v_s, pt_s, mixed_s, hidden_s, slope_s = saved
    slots, rows, width = local_rows.shape
    width, units, groups, lanes, chunk = sizes(params, rows)
    heads = width // HEAD
    per = heads // groups
    in_specs = [
        slot_whole(rows, width), whole((rows, width)), slot_whole(rows, width), whole((1, width)), whole((1, width)),
        section_columns(width, lanes), section_columns(width, lanes, groups), section_columns(width, lanes, 2 * groups),
        section_rows(lanes, width), section_columns(width, chunk), section_rows(chunk, width),
    ] + [whole((rows, lanes))] * 3 + [
        slot_columns(rows, lanes), slot_columns(rows, lanes), slot_columns(rows, lanes),
        pl.BlockSpec((1, per, rows, rows), lambda g, s: (s[0], g, 0, 0)),
        slot_columns(rows, chunk),
    ]
    operands = [
        local_rows, arriving, x_s, gain_a, gain_b, w_qkv, w_qkv, w_qkv, w_proj, w_up, w_down,
    ] + list(tables) + [q_s, k_s, v_s, pt_s, slope_s]
    out_specs = [
        whole((rows, width)), slot_whole(rows, width),
        slot_columns(rows, lanes), slot_columns(rows, lanes), slot_columns(rows, lanes), slot_columns(rows, chunk),
        slot_whole(8, width),
    ]
    out_shape = [jax.ShapeDtypeStruct((rows, width), BF16)] + [jax.ShapeDtypeStruct((slots, rows, width), BF16)] * 4 + [
        jax.ShapeDtypeStruct((slots, rows, units), BF16),
        jax.ShapeDtypeStruct((slots, 8, width), F32),
    ]
    aliases = {}
    kernel = functools.partial(backward_kernel, groups)
    if grads is not None:
        count = len(operands)
        inner = kernel

        def kernel(scalars, *refs):
            return inner(scalars, *refs[:count], *refs[count + len(grads):])

        in_specs = in_specs + [pl.BlockSpec(memory_space=pl.ANY)] * len(grads)
        operands = operands + list(grads)
        aliases = {1 + count + i: 1 + i for i in range(len(grads))}
    outs = pl.pallas_call(
        kernel,
        grid_spec=pltpu.PrefetchScalarGridSpec(
            num_scalar_prefetch=1, grid=(groups,), in_specs=in_specs, out_specs=out_specs,
            scratch_shapes=[pltpu.VMEM((rows, width), F32)] * 2,
        ),
        out_shape=out_shape,
        input_output_aliases=aliases,
        compiler_params=pltpu.CompilerParams(vmem_limit_bytes=VMEM_BYTES),
        cost_estimate=pl.CostEstimate(flops=2 * rows * (4 * width * width + 2 * width * units), bytes_accessed=22 << 20, transcendentals=0),
        name="layer_backward",
    )(scalars, *operands)
    return outs[0], outs[1:]


def place(scratch, parts, chunk_count, first_bit, mine):
    rows = sum(part.shape[0] for part in parts[0])
    half = chunk_count // 2
    for chunk in range(chunk_count):
        rest = (chunk >> (first_bit + 1) << first_bit) | (chunk & ((1 << first_bit) - 1))
        side = ((chunk >> first_bit) & 1) ^ mine
        start = pl.multiple_of(side * (half * rows) + rest * rows, 16)
        for part in parts[chunk]:
            scratch[pl.ds(start, part.shape[0]), :] = part
            start = pl.multiple_of(start + part.shape[0], 16)


def ones_dot(values):
    return dot(jnp.ones((16, values.shape[0]), BF16), values)[:8]


def down_proj_kernel(chunks, bit, scalars, hidden, mixed, gy, keep_out, send_out, sums_out, mixed_t, left):
    step = pl.program_id(0)
    rows = gy.shape[0] * gy.shape[1]
    grad = gy[...].reshape(rows, gy.shape[2])

    @pl.when(step == 0)
    def _():
        mixed_t[...] = mixed[...].reshape(rows, mixed.shape[2]).T
        sums_out[...] = ones_dot(grad)

    hidden_t = hidden[...].reshape(rows, hidden.shape[2]).T
    proj_rows = mixed_t.shape[0] // pl.num_programs(0)
    part_t = mixed_t[pl.ds(pl.multiple_of(step * proj_rows, 16), proj_rows), :]
    tall, low = hidden_t.shape[0] // chunks, proj_rows // chunks
    place(
        left,
        [[hidden_t[c * tall : c * tall + tall], part_t[c * low : c * low + low]] for c in range(chunks)],
        chunks, bit, scalars[bit],
    )
    product = dot(left[...], grad).astype(BF16)
    half = product.shape[0] // 2
    keep_out[...] = product[:half].reshape(keep_out.shape)
    send_out[...] = product[half:].reshape(send_out.shape)


def column_kernel(chunk_count, bit, scalars, normed, grad_refs, keep_out, send_out, sums_out, left):
    step = pl.program_id(0)
    rows = normed.shape[0] * normed.shape[1]

    @pl.when(step == 0)
    def _():
        normed_t = normed[...].reshape(rows, normed.shape[2]).T
        low = normed_t.shape[0] // chunk_count
        place(left, [[normed_t[c * low : c * low + low]] for c in range(chunk_count)], chunk_count, bit, scalars[bit])

    def emit(grad_ref):
        grad = grad_ref[...].reshape(rows, grad_ref.shape[2])
        product = dot(left[...], grad).astype(BF16)
        half = product.shape[0] // 2
        keep_out[...] = product[:half].reshape(keep_out.shape)
        send_out[...] = product[half:].reshape(send_out.shape)
        sums_out[...] = ones_dot(grad)

    if len(grad_refs) == 1:
        emit(grad_refs[0])
    else:
        for index, grad_ref in enumerate(grad_refs):
            pl.when(step == index)(functools.partial(emit, grad_ref))


def weight_call(kernel, grid, scalars, operands, in_specs, out_specs, out_shape, scratch, flops, name):
    return pl.pallas_call(
        kernel,
        grid_spec=pltpu.PrefetchScalarGridSpec(
            num_scalar_prefetch=1, grid=(grid,), in_specs=in_specs, out_specs=out_specs, scratch_shapes=scratch
        ),
        out_shape=out_shape,
        compiler_params=pltpu.CompilerParams(vmem_limit_bytes=VMEM_BYTES),
        cost_estimate=pl.CostEstimate(flops=flops, bytes_accessed=8 << 20, transcendentals=0),
        name=name,
    )(scalars, *operands)


def down_proj_grads(scalars, hidden, mixed, gy, count, bit):
    slots, rows, units = hidden.shape
    width = gy.shape[2]
    steps = 4
    chunks = count // steps
    tall = units // count + width // count
    out = jax.ShapeDtypeStruct((count // 2, tall, width), BF16)
    block = pl.BlockSpec((chunks // 2, tall, width), lambda g, s: (g, 0, 0))
    return weight_call(
        functools.partial(down_proj_kernel, chunks, bit), steps, scalars, [hidden, mixed, gy],
        [pl.BlockSpec((slots, rows, units // steps), lambda g, s: (0, 0, g)), whole((slots, rows, width)), whole((slots, rows, width))],
        [block, block, whole((8, width))],
        [out, out, jax.ShapeDtypeStruct((8, width), F32)],
        [pltpu.VMEM((width, slots * rows), BF16), pltpu.VMEM((chunks * tall, slots * rows), BF16)],
        2 * slots * rows * width * (units + width), "down_proj_grads",
    )


def column_grads(scalars, normed, grads, columns, count, bit, name):
    slots, rows, width = normed.shape
    total = sum(grad.shape[2] for grad in grads)
    low = width // count
    out = jax.ShapeDtypeStruct((count // 2, low, total), BF16)
    block = pl.BlockSpec((count // 2, low, columns), lambda g, s: (0, 0, g))
    if len(grads) == 1:
        specs = [pl.BlockSpec((slots, rows, columns), lambda g, s: (0, 0, g))]
    else:
        specs = [whole((slots, rows, columns))] * len(grads)

    def kernel(scalars_ref, normed_ref, *refs):
        column_kernel(count, bit, scalars_ref, normed_ref, refs[: len(grads)], *refs[len(grads) :])

    return weight_call(
        kernel, total // columns, scalars, [normed] + list(grads), [whole((slots, rows, width))] + specs,
        [block, block, pl.BlockSpec((8, columns), lambda g, s: (0, g))],
        [out, out, jax.ShapeDtypeStruct((8, total), F32)],
        [pltpu.VMEM((width, slots * rows), BF16)],
        2 * slots * rows * width * total, name,
    )


def swap(shard, bit, count):
    return lax.ppermute(shard, "dp", [(i, i ^ (1 << bit)) for i in range(count)])


def parted(values, position, mine):
    count = values.shape[0]
    shaped = values.reshape((count >> (position + 1), 2, 1 << position) + values.shape[1:])
    out = []
    for side in (mine, 1 - mine):
        piece = lax.dynamic_index_in_dim(shaped, side, axis=1, keepdims=False)
        out.append(piece.reshape((count // 2,) + values.shape[1:]))
    return out


def halving_sum(keep, send, order, count, bits, final):
    left = sorted(order)
    for number, bit in enumerate(order):
        left.remove(bit)
        arrived = swap(send, bit, count)
        if number + 1 == len(order):
            return (keep.astype(F32) + arrived.astype(F32)).astype(final)[0]
        position = left.index(order[number + 1])
        keep_a, send_a = parted(keep, position, bits[order[number + 1]])
        keep_b, send_b = parted(arrived, position, bits[order[number + 1]])
        send = (send_a.astype(F32) + send_b.astype(F32)).astype(send_a.dtype)
        keep = (keep_a.astype(F32) + keep_b.astype(F32)).astype(send_a.dtype)


def plain_grads(left, right, count):
    rows = left.shape[0] * left.shape[1]
    product = lax.dot_general(
        left.reshape(rows, -1), right.reshape(rows, -1), (((0,), (0,)), ((), ())), preferred_element_type=F32
    ).astype(BF16)
    return product.reshape(count, product.shape[0] // count, product.shape[1])


def column_sums(values):
    return jnp.sum(values, axis=(0, 1), dtype=F32)


def per_device(boundary, lengths, *params):
    section = lax.axis_index("section")
    count = lax.axis_size("dp")
    place_in = lax.axis_index("dp")
    bit_count = count.bit_length() - 1
    bits = [(place_in >> b) & 1 for b in range(bit_count)]
    slots = lengths.shape[0]
    width = boundary.shape[2]
    rows = boundary.shape[1] // slots
    units = params[8].shape[2]
    local_rows = boundary.reshape(slots, rows, width)
    ticks = slots + 1
    forward_slots = [jnp.clip(t - section, 0, slots - 1) for t in range(ticks)]
    backward_slots = [jnp.clip(t - 1 + section, 0, slots - 1) for t in range(ticks)]
    flag = (section == 0).astype(jnp.int32)
    tables = [jnp.asarray(table) for table in rotary_lanes(rows, 256)]

    def tick_scalars(slot):
        return jnp.stack([slot, flag, lengths[slot]]).astype(jnp.int32)

    swapped = [(0, 1), (1, 0)]
    arriving = jnp.zeros((rows, width), BF16)
    saved = None
    finals = []
    for t in range(ticks):
        result, saved = forward_tick(tick_scalars(forward_slots[t]), local_rows, arriving, params, tables, saved)
        finals.append(result)
        if t + 1 < ticks:
            arriving = lax.ppermute(result, "section", swapped)
    x_s, na_s, nb_s, q_s, k_s, v_s, pt_s, mixed_s, hidden_s, slope_s = saved
    grads = None
    input_grads = []
    arriving = jnp.zeros((rows, width), BF16)
    for t in range(ticks):
        result, grads = backward_tick(tick_scalars(backward_slots[t]), local_rows, arriving, params, tables, saved, grads)
        input_grads.append(result)
        if t + 1 < ticks:
            arriving = lax.ppermute(result, "section", swapped)
    gy_s, gq_s, gk_s, gv_s, gu_s, vec_s = grads

    orders = {
        "down": [1, 0] + list(range(2, bit_count)),
        "up": list(range(bit_count)),
        "qkv": list(range(2, bit_count)) + [0, 1],
    }
    bit_scalars = jnp.stack(bits).astype(jnp.int32)
    if (width // count) % 16 == 0:
        down_keep, down_send, gy_sums = down_proj_grads(bit_scalars, hidden_s, mixed_s, gy_s, count, orders["down"][0])
        up_keep, up_send, gu_sums = column_grads(bit_scalars, nb_s, [gu_s], units // 3, count, orders["up"][0], "up_grads")
        qkv_keep, qkv_send, gp_sums = column_grads(
            bit_scalars, na_s, [gq_s, gk_s, gv_s], width, count, orders["qkv"][0], "qkv_grads"
        )
        gy_sums, gu_sums, gp_sums = gy_sums[0], gu_sums[0], gp_sums[0]
    else:
        down_full = jnp.concatenate([plain_grads(hidden_s, gy_s, count), plain_grads(mixed_s, gy_s, count)], axis=1)
        down_keep, down_send = parted(down_full, orders["down"][0], bits[orders["down"][0]])
        up_keep, up_send = parted(plain_grads(nb_s, gu_s, count), orders["up"][0], bits[orders["up"][0]])
        gp_s = jnp.concatenate([gq_s, gk_s, gv_s], axis=2)
        qkv_keep, qkv_send = parted(plain_grads(na_s, gp_s, count), orders["qkv"][0], bits[orders["qkv"][0]])
        gy_sums, gu_sums, gp_sums = column_sums(gy_s), column_sums(gu_s), column_sums(gp_s)

    vec = jnp.sum(vec_s, axis=0)
    small = jnp.concatenate(
        [piece.reshape(count, -1) for piece in (vec[0], vec[1], vec[2], vec[3], gy_sums, gu_sums, gp_sums)], axis=1
    )
    small_keep, small_send = parted(small, orders["up"][0], bits[orders["up"][0]])

    down = halving_sum(down_keep, down_send, orders["down"], count, bits, F32)
    up = halving_sum(up_keep, up_send, orders["up"], count, bits, F32)
    qkv = halving_sum(qkv_keep, qkv_send, orders["qkv"], count, bits, F32)
    small = halving_sum(small_keep, small_send, orders["up"], count, bits, F32)
    low, tall = width // count, units // count
    cuts = np.cumsum([low] * 5 + [tall])
    gain_a, shift_a, gain_b, shift_b, bias_y, bias_up, bias_qkv = jnp.split(small, cuts, axis=0)
    joined = jnp.where(section == 0, jnp.concatenate(input_grads[1:], axis=0), jnp.concatenate(finals[1:], axis=0))
    results = (joined, gain_a, shift_a, qkv, bias_qkv, down[tall:], bias_y, gain_b, shift_b, up, bias_up, down[:tall], bias_y)
    return tuple(result[None] for result in results)


def solution(mesh):
    split = P("section", "dp")
    deep = P("section", "dp", None)
    flat, matrix = P("section", None), P("section", None, None)
    return jax.shard_map(
        per_device,
        mesh=mesh,
        in_specs=(deep, P("dp"), flat, flat, matrix, flat, matrix, flat, flat, flat, matrix, flat, matrix, flat),
        out_specs=(deep, split, split, deep, split, deep, split, split, split, deep, split, deep, split),
        check_vma=False,
    )
```

time: 852 us -> 327 us (0.38)
  waiting for transfers between devices: 448 us -> 143 us
  matrix products: 163 us -> 0 us
  Pallas kernels: 0 us -> 121 us
  blocking collectives: 79.5 us -> 0 us
  local copies, waits for them, and re-layouts: 67 us -> 13.9 us
  other arithmetic: 54.7 us -> 25.1 us
  between operations: 22.6 us -> 0.9 us
  starting transfers between devices: 9.6 us -> 22.6 us
    reduce_scatter x4 -> x0, waiting for transfers between devices: 446 us -> none  [the longest x1 177 us: per_device(): lax.psum_scatter(totals[10], 'dp', scatter_dimension=0, tiled=True)]
    dot_general x63 -> x0, matrix products: 163 us -> none  [the longest x15 63 us: matmul(): return jnp.dot(left, right, preferred_element_type=jnp.float32)]
    ppermute x4 -> x20, waiting for transfers between devices: 1.35 us -> 143 us  [the longest x16 142 us: swap(): return lax.ppermute(shard, 'dp', [(i, i ^ 1 << bit) for i in range(count)])]
    pallas_call x0 -> x9, Pallas kernels: none -> 121 us  [the longest x3 52.3 us: forward_tick(): pl.pallas_call(kernel, grid_spec=pltpu.PrefetchScalarGridSpec(num_scalar_...]
    unnamed x1 -> x0, blocking collectives: 79.5 us -> none
    add x7 -> x0, local copies, waits for them, and re-layouts: 20 us -> none  [the longest x6 18.6 us: layer_forward(): matmul(normed_a, weight_qkv) + bias_qkv.astype(jnp.float32)]
    reduce_sum x20 -> x1, other arithmetic: 18.4 us -> 0.01 us  [per_device(): vec = jnp.sum(vec_s, axis=0)]
    ppermute x4 -> x20, starting transfers between devices: 9.06 us -> 22.6 us  [the longest x16 21.2 us: swap(): return lax.ppermute(shard, 'dp', [(i, i ^ 1 << bit) for i in range(count)])]
  transfers between devices with their start and end apart: 8 -> 20, of which waited for: 4 -> 9; matrix products, arithmetic and copies ran while one was open for 14% -> 9% of each run, Pallas kernels for 0% -> 5%
where the time goes in v1:
time: 327 us; the launch traced here: 326 us
  waiting for transfers between devices  143 us (44%)
  Pallas kernels  121 us (37%)
  other arithmetic  25.1 us (8%)
  starting transfers between devices  22.6 us (7%)
  local copies, waits for them, and re-layouts  13.9 us (4%)
    ppermute x16, waiting for transfers between devices, swap(): return lax.ppermute(shard, 'dp', [(i, i ^ 1 << bit) for i in range(count)])  142 us
    pallas_call x3, Pallas kernels, forward_tick(): pl.pallas_call(kernel, grid_spec=pltpu.PrefetchScalarGridSpec(num_scalar_...  52.3 us
    pallas_call x3, Pallas kernels, backward_tick(): pl.pallas_call(kernel, grid_spec=pltpu.PrefetchScalarGridSpec(num_scalar_...  45.1 us
    pallas_call x3, Pallas kernels, weight_call(): pl.pallas_call(kernel, grid_spec=pltpu.PrefetchScalarGridSpec(num_scalar_...  23.1 us
    ppermute x16, starting transfers between devices, swap(): return lax.ppermute(shard, 'dp', [(i, i ^ 1 << bit) for i in range(count)])  21.2 us
    convert_element_type x6, other arithmetic, halving_sum(): keep = (keep_a.astype(F32) + keep_b.astype(F32)).astype(send_a.dtype)  12.6 us
    another operation x6, other arithmetic, tick_scalars(): return jnp.stack([slot, flag, lengths[slot]]).astype(jnp.int32)  7.38 us
  transfers between devices with their start and end apart: 20, of which 9 were waited for; matrix products, arithmetic and copies ran while one was open for 9% of the time, Pallas kernels for 5%

profile of v1, /device:TPU:0, one launch (start us, length us, event | category | flops | bytes accessed | tf_op | source)
XLA Modules:
  0.0 326.0 jit_solution(9046288842800029522)
XLA Ops:
  0.7 1.6 fusion.22
  2.2 1.2 pad_add_fusion.4.scalars
  3.5 0.8 broadcast_1_arriving.2.arriving
  4.2 17.4 %layer_forward.3 = (bf16[256,768]{1,0:T(8,128)(2,1)}, bf16[2,256,768]{2,1,0:T(8,128)(2,1)}, bf16[2,256,768]{2,1,0:T(8,128)(2,1)}, bf16[2,256,768]{2,1,0:T(8,128)...) custom-call(s32[3]{0:T(128)} %pad_add_fusion.4.scalars, ...), custom_call_target="tpu_custom_call" | custom-call | flops 3623878656 | bytes 23068672 | tf_op jit(solution)/shard_map/layer_forward/pallas_call | solution.py:267
  22.2 1.2 pad_add_fusion.3.scalars
  24.5 17.5 %layer_forward.4 = (bf16[256,768]{1,0:T(8,128)(2,1)}, bf16[2,256,768]{2,1,0:T(8,128)(2,1)}, bf16[2,256,768]{2,1,0:T(8,128)(2,1)}, bf16[2,256,768]{2,1,0:T(8,128)...) custom-call(s32[3]{0:T(128)} %pad_add_fusion.3.scalars, ...), custom_call_target="tpu_custom_call", output_to_operand_aliasing={{1}: (22, {}), {2}: (23, {}), {3}: (24, {}), {4}: (25, {}),... | custom-call | flops 3623878656 | bytes 23068672 | tf_op jit(solution)/shard_map/layer_forward/pallas_call | solution.py:267
  42.3 1.3 pad_add_fusion.1.scalars
  43.6 1.2 pad_add_fusion.2.scalars
  44.8 0.7 copy-done.4
  45.6 17.5 %layer_forward.5 = (bf16[256,768]{1,0:T(8,128)(2,1)}, bf16[2,256,768]{2,1,0:T(8,128)(2,1)}, bf16[2,256,768]{2,1,0:T(8,128)(2,1)}, bf16[2,256,768]{2,1,0:T(8,128)...) custom-call(s32[3]{0:T(128)} %pad_add_fusion.2.scalars, ...), custom_call_target="tpu_custom_call", output_to_operand_aliasing={{1}: (22, {}), {2}: (23, {}), {3}: (24, {}), {4}: (25, {}),... | custom-call | flops 3623878656 | bytes 23068672 | tf_op jit(solution)/shard_map/layer_forward/pallas_call | solution.py:267
  63.1 15.2 %layer_backward.3 = (bf16[256,768]{1,0:T(8,128)(2,1)}, bf16[2,256,768]{2,1,0:T(8,128)(2,1)}, bf16[2,256,768]{2,1,0:T(8,128)(2,1)}, bf16[2,256,768]{2,1,0:T(8,128...) custom-call(s32[3]{0:T(128)} %pad_add_fusion.1.scalars, ...), custom_call_target="tpu_custom_call" | custom-call | flops 3623878656 | bytes 23068672 | tf_op jit(solution)/shard_map/layer_backward/pallas_call | solution.py:322
  78.5 1.2 pad_add_fusion.scalars
  81.0 14.9 %layer_backward.4 = (bf16[256,768]{1,0:T(8,128)(2,1)}, bf16[2,256,768]{2,1,0:T(8,128)(2,1)}, bf16[2,256,768]{2,1,0:T(8,128)(2,1)}, bf16[2,256,768]{2,1,0:T(8,128...) custom-call(s32[3]{0:T(128)} %pad_add_fusion.scalars, ...), custom_call_target="tpu_custom_call", output_to_operand_aliasing={{1}: (20, {}), {2}: (21, {}), {3}: (22, {}), {4}: (23, {}),... | custom-call | flops 3623878656 | bytes 23068672 | tf_op jit(solution)/shard_map/layer_backward/pallas_call | solution.py:322
  96.2 1.2 pad_add_fusion.5.scalars
  98.0 0.7 copy-done.3
  98.7 15.0 %layer_backward.5 = (bf16[256,768]{1,0:T(8,128)(2,1)}, bf16[2,256,768]{2,1,0:T(8,128)(2,1)}, bf16[2,256,768]{2,1,0:T(8,128)(2,1)}, bf16[2,256,768]{2,1,0:T(8,128...) custom-call(s32[3]{0:T(128)} %pad_add_fusion.5.scalars, ...), custom_call_target="tpu_custom_call", output_to_operand_aliasing={{1}: (20, {}), {2}: (21, {}), {3}: (22, {}), {4}: (23, {}),... | custom-call | flops 3623878656 | bytes 23068672 | tf_op jit(solution)/shard_map/layer_backward/pallas_call | solution.py:322
  113.8 6.8 %qkv_grads.1 = (bf16[8,48,2304]{2,1,0:T(8,128)(2,1)}, bf16[8,48,2304]{2,1,0:T(8,128)(2,1)}, f32[8,2304]{1,0:T(8,128)}) custom-call(s32[4]{0:T(128)} %pad_add_fusion.6.scalars.scalars_ref, bf16[2,256,768]{2,1,0:T(8,128)(2,1)} %get-tuple-element.128.normed_ref, bf16[2,256,768]{2,1,0:T(8,128)(2,1)} %get-tuple-element.129.refs_0_, ...), custom_call_target="tpu_custom_call" | custom-call | flops 1811939328 | bytes 8388608 | tf_op jit(solution)/shard_map/qkv_grads/pallas_call | solution.py:404
  120.6 3.0 collective-permute-start.8
  123.6 7.2 %up_grads.1 = (bf16[8,48,3072]{2,1,0:T(8,128)(2,1)}, bf16[8,48,3072]{2,1,0:T(8,128)(2,1)}, f32[8,3072]{1,0:T(8,128)}) custom-call(s32[4]{0:T(128)} %pad_add_fusion.6.scalars.scalars_ref, bf16[2,256,768]{2,1,0:T(8,128)(2,1)} %get-tuple-element.125.normed_ref, bf16[2,256,3072]{2,1,0:T(8,128)(2,1)} %get-tuple-element.126.refs_0_), custom_call_target="tpu_custom_call" | custom-call | flops 2415919104 | bytes 8388608 | tf_op jit(solution)/shard_map/up_grads/pallas_call | solution.py:404
  130.8 1.5 collective-permute-start.16
  132.3 9.1 %down_proj_grads.1 = (bf16[8,240,768]{2,1,0:T(8,128)(2,1)}, bf16[8,240,768]{2,1,0:T(8,128)(2,1)}, f32[8,768]{1,0:T(8,128)}) custom-call(s32[4]{0:T(128)} %pad_add_fusion.6.scalars.scalars_ref, bf16[2,256,3072]{2,1,0:T(8,128)(2,1)} %get-tuple-element.121.hidden, bf16[2,256,768]{2,1,0:T(8,128)(2,1)} %get-tuple-element.122.mixed, ...), custom_call_target="tpu_custom_call" | custom-call | flops 3019898880 | bytes 8388608 | tf_op jit(solution)/shard_map/down_proj_grads/pallas_call | solution.py:404
  141.3 1.5 collective-permute-start.12
  143.2 0.8 slice_reduce_fusion.6
  144.1 0.9 slice_reduce_fusion
  145.1 0.9 slice_reduce_fusion.1
  147.0 37.5 %collective-permute-done.4 = f32[8,576]{1,0:T(8,128)S(1)} collective-permute-done((f32[8,576]{1,0:T(8,128)S(1)}, f32[8,576]{1,0:T(8,128)S(1)}, u32[]{:S(2)}, u32[]{:S(2)}) %collective-permute-start.4) | collective-permute-done | bytes 18464 | tf_op jit(solution)/shard_map/ppermute | solution.py:458
  184.5 1.2 copy-done.1
  185.7 3.4 %add_convert_fusion.5 = (bf16[1,1,4,48,2304]{4,3,2,1,0:T(8,128)(2,1)S(1)}, bf16[4,48,2304]{2,1,0:T(8,128)(2,1)}) fusion(bf16[1,2,4,48,2304]{4,3,2,1,0:T(8,128)(2,1)} %bitcast.91, s32[]{:T(128)S(6)} %select_n.107, bf16[1,2,4,48,2304]{4,3,2,1,0:T(8,128)(2,1)} %bitcast.90, s32[]{:T(128)S(6)} %select_n.109), kind=kLoop, calls=%fused_computation.5 | loop fusion | flops 3538944 | bytes 5308424 | tf_op jit(solution)/shard_map/convert_element_type | solution.py:482
  189.1 2.6 collective-permute-start.9
  191.7 3.6 %add_convert_fusion.3 = (bf16[4,1,1,48,3072]{4,3,1,0,2:T(8,128)(2,1)S(1)}, bf16[4,48,3072]{2,1,0:T(8,128)(2,1)}) fusion(bf16[4,2,1,48,3072]{4,3,1,0,2:T(8,128)(2,1)} %bitcast.37, s32[]{:T(128)S(6)} %select_n.103, bf16[4,2,1,48,3072]{4,3,1,0,2:T(8,128)(2,1)S(1)} %bitcast.89, s32[]{:T(128)S(6)} %select_n.106), kind=kLoop, calls=%fused_computation.3 | loop fusion | flops 4718592 | bytes 7077896 | tf_op jit(solution)/shard_map/convert_element_type | solution.py:482
  195.3 1.5 collective-permute-start.17
  197.4 35.0 %collective-permute-done.5 = f32[4,576]{1,0:T(4,128)S(1)} collective-permute-done((f32[4,576]{1,0:T(4,128)S(1)}, f32[4,576]{1,0:T(4,128)S(1)}, u32[]{:S(2)}, u32[]{:S(2)}) %collective-permute-start.5) | collective-permute-done | bytes 9248 | tf_op jit(solution)/shard_map/ppermute | solution.py:458
  233.0 2.4 maximum_select_fusion
  235.4 0.8 collective-permute-done.6
  236.2 2.7 collective-permute-start.7
  238.8 3.4 %add_convert_fusion.1 = (bf16[4,1,1,240,768]{4,3,1,0,2:T(8,128)(2,1)S(1)}, bf16[4,240,768]{2,1,0:T(8,128)(2,1)S(1)}) fusion(bf16[4,2,1,240,768]{4,3,1,0,2:T(8,128)(2,1)} %bitcast.29, s32[]{:T(128)S(6)} %select_n.102, bf16[4,2,1,240,768]{4,3,1,0,2:T(8,128)(2,1)} %bitcast.88, s32[]{:T(128)S(6)} %select_n.104), kind=kLoop, calls=%fused_computation.1 | loop fusion | flops 5898240 | bytes 8847368 | tf_op jit(solution)/shard_map/convert_element_type | solution.py:482
  244.1 1.4 add_convert_fusion.11
  245.5 1.6 collective-permute-start.10
  247.4 0.9 collective-permute-start.18
  248.9 34.4 %collective-permute-done.10 = bf16[2,48,2304]{2,1,0:T(8,128)(2,1)S(1)} collective-permute-done((bf16[2,48,2304]{2,1,0:T(8,128)(2,1)S(1)}, bf16[2,48,2304]{2,1,0:T(8,128)(2,1)S(1)}, u32[]{:S(2)}, u32[]{:S(2)}) %collective-permute-start.10) | collective-permute-done | bytes 442400 | tf_op jit(solution)/shard_map/ppermute | solution.py:458
  283.4 1.6 collective-permute-start.11
  285.4 1.6 collective-permute-start.14
  287.5 1.9 collective-permute-done.11
  289.4 0.8 convert_add_fusion.8
  290.2 16.7 %collective-permute-done.14 = bf16[2,240,768]{2,1,0:T(8,128)(2,1)S(1)} collective-permute-done((bf16[2,240,768]{2,1,0:T(8,128)(2,1)S(1)}, bf16[2,240,768]{2,1,0:T(8,128)(2,1)S(1)}, u32[]{:S(2)}, u32[]{:S(2)}) %collective-permute-start.14) | collective-permute-done | bytes 737312 | tf_op jit(solution)/shard_map/ppermute | solution.py:458
  307.1 0.9 convert_add_fusion.5
  308.0 15.8 %collective-permute-done.15 = bf16[1,240,768]{2,1,0:T(8,128)(2,1)S(1)} collective-permute-done((bf16[1,240,768]{2,1,0:T(8,128)(2,1)S(1)}, bf16[1,240,768]{2,1,0:T(8,128)(2,1)S(1)}, u32[]{:S(2)}, u32[]{:S(2)}) %collective-permute-start.15) | collective-permute-done | bytes 368672 | tf_op jit(solution)/shard_map/ppermute | solution.py:458
  324.6 0.9 slice.50
  (68 shorter events, 12.4 us)
Async XLA Ops:
  21.6 2.1 collective-permute-start
  23.7 0.7 copy-start.5
  41.9 2.9 collective-permute-start.1
  44.8 0.7 copy-start.4
  78.2 2.0 collective-permute-start.2
  80.2 0.7 copy-start.6
  95.9 2.1 collective-permute-start.3
  98.0 0.7 copy-start.3
  120.6 63.9 %collective-permute-start.8 = (bf16[8,48,2304]{2,1,0:T(8,128)(2,1)}, bf16[8,48,2304]{2,1,0:T(8,128)(2,1)S(1)}, u32[]{:S(2)}, u32[]{:S(2)}) collective-permute-start(bf16[8,48,2304]{2,1,0:T(8,128)(2,1)} %get-tuple-element.134), channel_id=1, source_target_pairs={{0,4},{1,5},{2,6},{3,7},{4,0},{5,1},{6,2},{7,3},{8,12},{9,13},{10,... | collective-permute-start | bytes 5308424 | tf_op jit(solution)/shard_map/ppermute | solution.py:458
  130.8 60.9 %collective-permute-start.16 = (bf16[8,48,3072]{2,1,0:T(8,128)(2,1)}, bf16[8,48,3072]{2,1,0:T(8,128)(2,1)}, u32[]{:S(2)}, u32[]{:S(2)}) collective-permute-start(bf16[8,48,3072]{2,1,0:T(8,128)(2,1)} %get-tuple-element.138), channel_id=1, source_target_pairs={{0,1},{1,0},{2,3},{3,2},{4,5},{5,4},{6,7},{7,6},{8,9},{9,8},{10,11... | collective-permute-start | bytes 7077896 | tf_op jit(solution)/shard_map/ppermute | solution.py:458
  132.3 10.6 %copy-start.2 = (f32[2,8,768]{2,1,0:T(8,128)S(1)}, f32[2,8,768]{2,1,0:T(8,128)}, u32[]{:S(2)}) copy-start(f32[2,8,768]{2,1,0:T(8,128)} %get-tuple-element.120) | copy-start | bytes 147460
  141.3 97.5 %collective-permute-start.12 = (bf16[8,240,768]{2,1,0:T(8,128)(2,1)}, bf16[8,240,768]{2,1,0:T(8,128)(2,1)}, u32[]{:S(2)}, u32[]{:S(2)}) collective-permute-start(bf16[8,240,768]{2,1,0:T(8,128)(2,1)} %get-tuple-element.136), channel_id=1, source_target_pairs={{0,2},{1,3},{2,0},{3,1},{4,6},{5,7},{6,4},{7,5},{8,10},{9,11},{10,... | collective-permute-start | bytes 8847368 | tf_op jit(solution)/shard_map/ppermute | solution.py:458
  146.4 38.1 %collective-permute-start.4 = (f32[8,576]{1,0:T(8,128)S(1)}, f32[8,576]{1,0:T(8,128)S(1)}, u32[]{:S(2)}, u32[]{:S(2)}) collective-permute-start(f32[8,576]{1,0:T(8,128)S(1)} %bitcast.100), channel_id=1, source_target_pairs={{0,1},{1,0},{2,3},{3,2},{4,5},{5,4},{6,7},{7,6},{8,9},{9,8},{10,11... | collective-permute-start | bytes 55304 | tf_op jit(solution)/shard_map/ppermute | solution.py:458
  184.5 1.2 copy-start.1
  185.7 6.0 %copy-start = (bf16[8,48,3072]{2,1,0:T(8,128)(2,1)S(1)}, bf16[8,48,3072]{2,1,0:T(8,128)(2,1)}, u32[]{:S(2)}) copy-start(bf16[8,48,3072]{2,1,0:T(8,128)(2,1)} %get-tuple-element.137) | copy-start | bytes 7077892
  189.1 55.0 %collective-permute-start.9 = (bf16[4,48,2304]{2,1,0:T(8,128)(2,1)}, bf16[4,48,2304]{2,1,0:T(8,128)(2,1)}, u32[]{:S(2)}, u32[]{:S(2)}) collective-permute-start(bf16[4,48,2304]{2,1,0:T(8,128)(2,1)} %get-tuple-element.148), channel_id=1, source_target_pairs={{0,8},{1,9},{2,10},{3,11},{4,12},{5,13},{6,14},{7,15},{8,0},{9,1},... | collective-permute-start | bytes 2654216 | tf_op jit(solution)/shard_map/ppermute | solution.py:458
  195.3 51.8 %collective-permute-start.17 = (bf16[4,48,3072]{2,1,0:T(8,128)(2,1)}, bf16[4,48,3072]{2,1,0:T(8,128)(2,1)S(1)}, u32[]{:S(2)}, u32[]{:S(2)}) collective-permute-start(bf16[4,48,3072]{2,1,0:T(8,128)(2,1)} %get-tuple-element.146), channel_id=1, source_target_pairs={{0,2},{1,3},{2,0},{3,1},{4,6},{5,7},{6,4},{7,5},{8,10},{9,11},{10,... | collective-permute-start | bytes 3538952 | tf_op jit(solution)/shard_map/ppermute | solution.py:458
  196.9 35.5 %collective-permute-start.5 = (f32[4,576]{1,0:T(4,128)S(1)}, f32[4,576]{1,0:T(4,128)S(1)}, u32[]{:S(2)}, u32[]{:S(2)}) collective-permute-start(f32[4,576]{1,0:T(4,128)S(1)} %bitcast.101), channel_id=1, source_target_pairs={{0,2},{1,3},{2,0},{3,1},{4,6},{5,7},{6,4},{7,5},{8,10},{9,11},{10,... | collective-permute-start | bytes 27656 | tf_op jit(solution)/shard_map/ppermute | solution.py:458
  232.5 3.7 %collective-permute-start.6 = (f32[2,576]{1,0:T(2,128)S(1)}, f32[2,576]{1,0:T(2,128)S(1)}, u32[]{:S(2)}, u32[]{:S(2)}) collective-permute-start(f32[2,576]{1,0:T(2,128)S(1)} %bitcast.102), channel_id=1, source_target_pairs={{0,4},{1,5},{2,6},{3,7},{4,0},{5,1},{6,2},{7,3},{8,12},{9,13},{10,... | collective-permute-start | bytes 13832 | tf_op jit(solution)/shard_map/ppermute | solution.py:458
  236.2 6.7 %collective-permute-start.7 = (f32[1,576]{1,0:T(1,128)S(1)}, f32[1,576]{1,0:T(1,128)S(1)}, u32[]{:S(2)}, u32[]{:S(2)}) collective-permute-start(f32[1,576]{1,0:T(1,128)S(1)} %fusion.20), channel_id=1, source_target_pairs={{0,8},{1,9},{2,10},{3,11},{4,12},{5,13},{6,14},{7,15},{8,0},{9,1},... | collective-permute-start | bytes 6920 | tf_op jit(solution)/shard_map/ppermute | solution.py:458
  242.2 42.7 %collective-permute-start.13 = (bf16[4,240,768]{2,1,0:T(8,128)(2,1)S(1)}, bf16[4,240,768]{2,1,0:T(8,128)(2,1)S(1)}, u32[]{:S(2)}, u32[]{:S(2)}) collective-permute-start(bf16[4,240,768]{2,1,0:T(8,128)(2,1)S(1)} %get-tuple-element.144), channel_id=1, source_target_pairs={{0,1},{1,0},{2,3},{3,2},{4,5},{5,4},{6,7},{7,6},{8,9},{9,8},{10,11... | collective-permute-start | bytes 4423688 | tf_op jit(solution)/shard_map/ppermute | solution.py:458
  245.5 37.8 %collective-permute-start.10 = (bf16[2,48,2304]{2,1,0:T(8,128)(2,1)S(1)}, bf16[2,48,2304]{2,1,0:T(8,128)(2,1)S(1)}, u32[]{:S(2)}, u32[]{:S(2)}) collective-permute-start(bf16[2,48,2304]{2,1,0:T(8,128)(2,1)S(1)} %get-tuple-element.154), channel_id=1, source_target_pairs={{0,1},{1,0},{2,3},{3,2},{4,5},{5,4},{6,7},{7,6},{8,9},{9,8},{10,11... | collective-permute-start | bytes 1327112 | tf_op jit(solution)/shard_map/ppermute | solution.py:458
  247.4 39.6 %collective-permute-start.18 = (bf16[2,48,3072]{2,1,0:T(8,128)(2,1)S(1)}, bf16[2,48,3072]{2,1,0:T(8,128)(2,1)S(1)}, u32[]{:S(2)}, u32[]{:S(2)}) collective-permute-start(bf16[2,48,3072]{2,1,0:T(8,128)(2,1)S(1)} %get-tuple-element.152), channel_id=1, source_target_pairs={{0,4},{1,5},{2,6},{3,7},{4,0},{5,1},{6,2},{7,3},{8,12},{9,13},{10,... | collective-permute-start | bytes 1769480 | tf_op jit(solution)/shard_map/ppermute | solution.py:458
  248.9 76.6 %copy-start.7 = (f32[1,48]{1,0:T(1,128)}, f32[1,48]{1,0:T(1,128)S(1)}, u32[]{:S(2)}) copy-start(f32[1,48]{1,0:T(1,128)S(1)} %get-tuple-element.197) | copy-start | bytes 580
  283.4 6.0 %collective-permute-start.11 = (bf16[1,48,2304]{2,1,0:T(8,128)(2,1)S(1)}, bf16[1,48,2304]{2,1,0:T(8,128)(2,1)S(1)}, u32[]{:S(2)}, u32[]{:S(2)}) collective-permute-start(bf16[1,48,2304]{2,1,0:T(8,128)(2,1)S(1)} %fusion.10), channel_id=1, source_target_pairs={{0,2},{1,3},{2,0},{3,1},{4,6},{5,7},{6,4},{7,5},{8,10},{9,11},{10,... | collective-permute-start | bytes 663560 | tf_op jit(solution)/shard_map/ppermute | solution.py:458
  285.4 21.5 %collective-permute-start.14 = (bf16[2,240,768]{2,1,0:T(8,128)(2,1)S(1)}, bf16[2,240,768]{2,1,0:T(8,128)(2,1)S(1)}, u32[]{:S(2)}, u32[]{:S(2)}) collective-permute-start(bf16[2,240,768]{2,1,0:T(8,128)(2,1)S(1)} %get-tuple-element.150), channel_id=1, source_target_pairs={{0,4},{1,5},{2,6},{3,7},{4,0},{5,1},{6,2},{7,3},{8,12},{9,13},{10,... | collective-permute-start | bytes 2211848 | tf_op jit(solution)/shard_map/ppermute | solution.py:458
  287.1 20.0 %collective-permute-start.19 = (bf16[1,48,3072]{2,1,0:T(8,128)(2,1)S(1)}, bf16[1,48,3072]{2,1,0:T(8,128)(2,1)S(1)}, u32[]{:S(2)}, u32[]{:S(2)}) collective-permute-start(bf16[1,48,3072]{2,1,0:T(8,128)(2,1)S(1)} %fusion.7), channel_id=1, source_target_pairs={{0,8},{1,9},{2,10},{3,11},{4,12},{5,13},{6,14},{7,15},{8,0},{9,1},... | collective-permute-start | bytes 884744 | tf_op jit(solution)/shard_map/ppermute | solution.py:458
  307.0 16.8 %collective-permute-start.15 = (bf16[1,240,768]{2,1,0:T(8,128)(2,1)S(1)}, bf16[1,240,768]{2,1,0:T(8,128)(2,1)S(1)}, u32[]{:S(2)}, u32[]{:S(2)}) collective-permute-start(bf16[1,240,768]{2,1,0:T(8,128)(2,1)S(1)} %fusion.4), channel_id=1, source_target_pairs={{0,8},{1,9},{2,10},{3,11},{4,12},{5,13},{6,14},{7,15},{8,0},{9,1},... | collective-permute-start | bytes 1105928 | tf_op jit(solution)/shard_map/ppermute | solution.py:458
